TPU v7x, 32 devices: a whole 2x2x4 slice. The times are simulated.
32 devices in a mesh: seq: 16 (over z, y, core), dp: 2 (over x).
Axes of the slice: x: 2, y: 2, z: 4, core: 2. Of those that a mesh axis runs over, the one named last changes fastest.
Arguments:
- tokens: float32 [32, 256, 1152], P(('seq', 'dp')), may hold values from -6 to 6
- condition: float32 [32, 1152], P(('seq', 'dp')), may hold values from -8 to 8
- kept_tokens: int32 [32, 256], P(('seq', 'dp')), may hold values from 0 to 1, as said below
- grad_out: float32 [32, 256, 1152], P(('seq', 'dp')), may hold values from -6 to 6
- entry_weight: float32 [1152, 3456], P('seq', 'dp'), may hold values from -0.1875 to 0.1875
- merge_weight: float32 [1152, 1152], P('seq', 'dp'), may hold values from -1 to 1
- expand_weight: float32 [1152, 4608], P('seq', 'dp'), may hold values from -0.1875 to 0.1875
- shrink_weight: float32 [4608, 1152], P('seq', 'dp'), may hold values from -0.09375 to 0.09375
- modulate_weight: float32 [1152, 6912], P('seq', 'dp'), may hold values from -0.1875 to 0.1875
- entry_velocity: float32 [1152, 3456], P('seq', 'dp'), may hold values from -160 to 160
- merge_velocity: float32 [1152, 1152], P('seq', 'dp'), may hold values from -160 to 160
- expand_velocity: float32 [1152, 4608], P('seq', 'dp'), may hold values from -160 to 160
- shrink_velocity: float32 [4608, 1152], P('seq', 'dp'), may hold values from -160 to 160
- modulate_velocity: float32 [1152, 6912], P('seq', 'dp'), may hold values from -160 to 160
- entry_average: float32 [1152, 3456], P('seq', 'dp'), may hold values from -0.1875 to 0.1875
- merge_average: float32 [1152, 1152], P('seq', 'dp'), may hold values from -1 to 1
- expand_average: float32 [1152, 4608], P('seq', 'dp'), may hold values from -0.1875 to 0.1875
- shrink_average: float32 [4608, 1152], P('seq', 'dp'), may hold values from -0.09375 to 0.09375
- modulate_average: float32 [1152, 6912], P('seq', 'dp'), may hold values from -0.1875 to 0.1875
Outputs:
- output: float32 [32, 256, 1152], P(('seq', 'dp'))
- grad_tokens: float32 [32, 256, 1152], P(('seq', 'dp'))
- entry_next: float32 [1152, 3456], P('seq', 'dp')
- merge_next: float32 [1152, 1152], P('seq', 'dp')
- expand_next: float32 [1152, 4608], P('seq', 'dp')
- shrink_next: float32 [4608, 1152], P('seq', 'dp')
- modulate_next: float32 [1152, 6912], P('seq', 'dp')
- entry_velocity_next: float32 [1152, 3456], P('seq', 'dp')
- merge_velocity_next: float32 [1152, 1152], P('seq', 'dp')
- expand_velocity_next: float32 [1152, 4608], P('seq', 'dp')
- shrink_velocity_next: float32 [4608, 1152], P('seq', 'dp')
- modulate_velocity_next: float32 [1152, 6912], P('seq', 'dp')
- entry_average_next: float32 [1152, 3456], P('seq', 'dp')
- merge_average_next: float32 [1152, 1152], P('seq', 'dp')
- expand_average_next: float32 [1152, 4608], P('seq', 'dp')
- shrink_average_next: float32 [4608, 1152], P('seq', 'dp')
- modulate_average_next: float32 [1152, 6912], P('seq', 'dp')
Inputs may be any that keep to these rules, and one draw needn't show every extreme that they name: `kept_tokens`: each latent keeps between 160 and 192 of its 256 slots, the number varying from latent to latent, the slots scattered at random.
All inputs are finite; a program needn't handle non-finite values.
Results may differ from a plain program's by a relative error of at most 0.02.
The roundings to bfloat16 on the way count: a program that leaves them out, or rounds other values in their place, can miss the bound.
Values may be sent and summed in bfloat16 or wider, within the bound.
No kernel may reach another device: no remote copies, remote signals or barrier semaphores. Data moves between devices by JAX's collectives and lax.ppermute only.
A program may use at most 192 MiB of HBM per device.

v0:
```python
import math

import jax
import jax.numpy as jnp
from jax import lax
from jax.sharding import PartitionSpec as P

HEADS = 16


EPSILON = 1e-06
DECAY = 0.5


def for_sending(x):
    return jax.tree.map(lambda a: a.astype(jnp.bfloat16) if a.dtype == jnp.float32 else a, x)


def normalize(values):
    average = jnp.mean(values, axis=-1, keepdims=True)
    centred = values - average
    inverse = lax.rsqrt(jnp.mean(centred * centred, axis=-1, keepdims=True) + EPSILON)
    return (centred * inverse, inverse)


def norm_back(gradient, normed, inverse):
    return inverse * (
        gradient
        - jnp.mean(gradient, axis=-1, keepdims=True)
        - normed * jnp.mean(gradient * normed, axis=-1, keepdims=True)
    )


def part_of(table, number):
    return table[:, number][:, None, :]


def attend(bundle):
    projected, kept_tokens = bundle
    length, triple = projected.shape
    model_width = triple // 3
    head_size = model_width // HEADS
    sections = projected.reshape(length, 3, HEADS, head_size)
    queries = sections[:, 0]
    keys_part = sections[:, 1]
    values = sections[:, 2]
    scale = 1.0 / math.sqrt(head_size)
    scores = (
        jnp.einsum("qhd,khd->hqk", queries, keys_part, preferred_element_type=jnp.float32) * scale
    )
    scores = jnp.where(kept_tokens[None, None, :] > 0, scores, -1000000000.0)
    row_max = jnp.max(scores, axis=-1, keepdims=True)
    exponent = jnp.exp(scores - row_max)
    row_sum = jnp.sum(exponent, axis=-1, keepdims=True)
    soft_weights = (exponent / row_sum).astype(jnp.bfloat16)
    attended = jnp.einsum("hqk,khd->qhd", soft_weights, values, preferred_element_type=jnp.float32)
    return (attended.astype(jnp.bfloat16).reshape(length, model_width), row_max + jnp.log(row_sum))


def attend_back(bundle):
    projected, kept_tokens, log_total, grad_attended = bundle
    length, triple = projected.shape
    model_width = triple // 3
    head_size = model_width // HEADS
    sections = projected.reshape(length, 3, HEADS, head_size)
    queries = sections[:, 0]
    keys_part = sections[:, 1]
    values = sections[:, 2]
    scale = 1.0 / math.sqrt(head_size)
    scores = (
        jnp.einsum("qhd,khd->hqk", queries, keys_part, preferred_element_type=jnp.float32) * scale
    )
    scores = jnp.where(kept_tokens[None, None, :] > 0, scores, -1000000000.0)
    soft_weights = jnp.exp(scores - log_total)
    upstream = grad_attended.reshape(length, HEADS, head_size)
    grad_soft = jnp.einsum("qhd,khd->hqk", upstream, values, preferred_element_type=jnp.float32)
    grad_scores = (
        soft_weights * (grad_soft - jnp.sum(soft_weights * grad_soft, axis=-1, keepdims=True))
    ).astype(jnp.bfloat16)
    grad_queries = (
        jnp.einsum("hqk,khd->qhd", grad_scores, keys_part, preferred_element_type=jnp.float32)
        * scale
    )
    grad_keys = (
        jnp.einsum("hqk,qhd->khd", grad_scores, queries, preferred_element_type=jnp.float32) * scale
    )
    grad_values = jnp.einsum(
        "hqk,qhd->khd",
        soft_weights.astype(jnp.bfloat16),
        upstream,
        preferred_element_type=jnp.float32,
    )
    stacked = jnp.stack([grad_queries, grad_keys, grad_values], axis=1).astype(jnp.bfloat16)
    return stacked.reshape(length, triple)


def forward_pass(tokens, condition, kept_tokens, full):
    entry, merge, expand, shrink, modulate = full
    latents, length, model_width = tokens.shape
    lifted = jax.nn.silu(condition).astype(jnp.bfloat16)
    table = jnp.dot(lifted, modulate, preferred_element_type=jnp.float32).reshape(
        latents, 6, model_width
    )
    shift_one, scale_one, gate_one, shift_two, scale_two, gate_two = [
        part_of(table, number) for number in range(6)
    ]
    kept_mask = kept_tokens.astype(jnp.float32)[:, :, None]
    normed_one, inverse_one = normalize(tokens)
    hidden_one = (normed_one * (1.0 + scale_one) + shift_one).astype(jnp.bfloat16)
    projected = jnp.dot(
        hidden_one.reshape(-1, model_width), entry, preferred_element_type=jnp.float32
    ).astype(jnp.bfloat16)
    projected = projected.reshape(latents, length, 3 * model_width)
    attended, log_total = lax.map(attend, (projected, kept_tokens))
    attention_out = jnp.dot(
        attended.reshape(-1, model_width), merge, preferred_element_type=jnp.float32
    ).reshape(latents, length, model_width)
    middle = tokens + kept_mask * gate_one * attention_out
    normed_two, inverse_two = normalize(middle)
    hidden_two = (normed_two * (1.0 + scale_two) + shift_two).astype(jnp.bfloat16)
    expanded = jnp.dot(
        hidden_two.reshape(-1, model_width), expand, preferred_element_type=jnp.float32
    )
    activated = jax.nn.gelu(expanded).astype(jnp.bfloat16)
    feed = jnp.dot(activated, shrink, preferred_element_type=jnp.float32).reshape(
        latents, length, model_width
    )
    result = middle + kept_mask * gate_two * feed
    saved = (
        lifted,
        table,
        kept_mask,
        normed_one,
        inverse_one,
        hidden_one,
        projected,
        attended,
        log_total,
        attention_out,
        middle,
        normed_two,
        inverse_two,
        hidden_two,
        expanded,
        activated,
        feed,
    )
    return (result, saved)


def local(
    tokens,
    condition,
    kept_tokens,
    grad_out,
    entry_weight,
    merge_weight,
    expand_weight,
    shrink_weight,
    modulate_weight,
    entry_velocity,
    merge_velocity,
    expand_velocity,
    shrink_velocity,
    modulate_velocity,
    entry_average,
    merge_average,
    expand_average,
    shrink_average,
    modulate_average,
):
    masters = (entry_weight, merge_weight, expand_weight, shrink_weight, modulate_weight)
    velocities = (
        entry_velocity,
        merge_velocity,
        expand_velocity,
        shrink_velocity,
        modulate_velocity,
    )
    averages = (entry_average, merge_average, expand_average, shrink_average, modulate_average)
    halves = tuple((master.astype(jnp.bfloat16) for master in masters))
    widened = jax.tree.map(
        lambda part, own: part.astype(own.dtype),
        lax.all_gather(for_sending(halves), "dp", axis=1, tiled=True),
        halves,
    )
    full = jax.tree.map(
        lambda part, own: part.astype(own.dtype),
        lax.all_gather(for_sending(widened), "seq", axis=0, tiled=True),
        widened,
    )
    result, unused = forward_pass(tokens, condition, kept_tokens, full)
    widened_again = jax.tree.map(
        lambda part, own: part.astype(own.dtype),
        lax.all_gather(for_sending(halves), "dp", axis=1, tiled=True),
        halves,
    )
    second = jax.tree.map(
        lambda part, own: part.astype(own.dtype),
        lax.all_gather(for_sending(widened_again), "seq", axis=0, tiled=True),
        widened_again,
    )
    entry, merge, expand, shrink, modulate = second
    again_result, saved = forward_pass(tokens, condition, kept_tokens, second)
    (
        lifted,
        table,
        kept_mask,
        normed_one,
        inverse_one,
        hidden_one,
        projected,
        attended,
        log_total,
        attention_out,
        middle,
        normed_two,
        inverse_two,
        hidden_two,
        expanded,
        activated,
        feed,
    ) = saved
    latents, length, model_width = tokens.shape
    row_count = latents * length
    scale_one = part_of(table, 1)
    gate_one = part_of(table, 2)
    scale_two = part_of(table, 4)
    gate_two = part_of(table, 5)
    grad_feed = (
        (kept_mask * gate_two * grad_out).astype(jnp.bfloat16).reshape(row_count, model_width)
    )
    grad_gate_two = jnp.sum(kept_mask * feed * grad_out, axis=1)
    grad_shrink = jnp.einsum("rf,rd->fd", activated, grad_feed, preferred_element_type=jnp.float32)
    grad_activated = jnp.einsum("rd,fd->rf", grad_feed, shrink, preferred_element_type=jnp.float32)
    grad_expanded = jax.vjp(jax.nn.gelu, expanded)[1](grad_activated)[0].astype(jnp.bfloat16)
    grad_expand = jnp.einsum(
        "rd,rf->df",
        hidden_two.reshape(row_count, model_width),
        grad_expanded,
        preferred_element_type=jnp.float32,
    )
    grad_hidden_two = jnp.einsum(
        "rf,df->rd", grad_expanded, expand, preferred_element_type=jnp.float32
    ).reshape(latents, length, model_width)
    grad_scale_two = jnp.sum(grad_hidden_two * normed_two, axis=1)
    grad_shift_two = jnp.sum(grad_hidden_two, axis=1)
    grad_middle = grad_out + norm_back(grad_hidden_two * (1.0 + scale_two), normed_two, inverse_two)
    grad_attention = (
        (kept_mask * gate_one * grad_middle).astype(jnp.bfloat16).reshape(row_count, model_width)
    )
    grad_gate_one = jnp.sum(kept_mask * attention_out * grad_middle, axis=1)
    grad_merge = jnp.einsum(
        "rc,rd->cd",
        attended.reshape(row_count, model_width),
        grad_attention,
        preferred_element_type=jnp.float32,
    )
    grad_attended = jnp.einsum(
        "rd,cd->rc", grad_attention, merge, preferred_element_type=jnp.float32
    ).astype(jnp.bfloat16)
    grad_attended = grad_attended.reshape(latents, length, model_width)
    grad_projected = lax.map(attend_back, (projected, kept_tokens, log_total, grad_attended))
    grad_projected = grad_projected.reshape(row_count, 3 * model_width)
    grad_entry = jnp.einsum(
        "rd,re->de",
        hidden_one.reshape(row_count, model_width),
        grad_projected,
        preferred_element_type=jnp.float32,
    )
    grad_hidden_one = jnp.einsum(
        "re,de->rd", grad_projected, entry, preferred_element_type=jnp.float32
    ).reshape(latents, length, model_width)
    grad_scale_one = jnp.sum(grad_hidden_one * normed_one, axis=1)
    grad_shift_one = jnp.sum(grad_hidden_one, axis=1)
    grad_tokens = grad_middle + norm_back(
        grad_hidden_one * (1.0 + scale_one), normed_one, inverse_one
    )
    grad_table = jnp.stack(
        [
            grad_shift_one,
            grad_scale_one,
            grad_gate_one,
            grad_shift_two,
            grad_scale_two,
            grad_gate_two,
        ],
        axis=1,
    )
    grad_table = grad_table.reshape(latents, 6 * model_width).astype(jnp.bfloat16)
    grad_modulate = jnp.einsum("ld,le->de", lifted, grad_table, preferred_element_type=jnp.float32)
    shards = (
        lax.psum_scatter(
            grad_entry.astype(jnp.bfloat16), "seq", scatter_dimension=0, tiled=True
        ).astype(jnp.float32),
        lax.psum_scatter(
            grad_merge.astype(jnp.bfloat16), "seq", scatter_dimension=0, tiled=True
        ).astype(jnp.float32),
        lax.psum_scatter(
            grad_expand.astype(jnp.bfloat16), "seq", scatter_dimension=0, tiled=True
        ).astype(jnp.float32),
        lax.psum_scatter(
            grad_shrink.astype(jnp.bfloat16), "seq", scatter_dimension=0, tiled=True
        ).astype(jnp.float32),
        lax.psum_scatter(
            grad_modulate.astype(jnp.bfloat16), "seq", scatter_dimension=0, tiled=True
        ).astype(jnp.float32),
    )
    summed = (
        lax.psum_scatter(
            shards[0].astype(jnp.bfloat16), "dp", scatter_dimension=1, tiled=True
        ).astype(jnp.float32),
        lax.psum_scatter(
            shards[1].astype(jnp.bfloat16), "dp", scatter_dimension=1, tiled=True
        ).astype(jnp.float32),
        lax.psum_scatter(
            shards[2].astype(jnp.bfloat16), "dp", scatter_dimension=1, tiled=True
        ).astype(jnp.float32),
        lax.psum_scatter(
            shards[3].astype(jnp.bfloat16), "dp", scatter_dimension=1, tiled=True
        ).astype(jnp.float32),
        lax.psum_scatter(
            shards[4].astype(jnp.bfloat16), "dp", scatter_dimension=1, tiled=True
        ).astype(jnp.float32),
    )
    total_rows = latents * length * lax.axis_size("seq") * lax.axis_size("dp")
    rate = 0.03 / math.sqrt(total_rows)
    moved_list = []
    velocity_list = []
    average_list = []
    for master, velocity, average, gradient in zip(masters, velocities, averages, summed):
        fresh_velocity = DECAY * velocity + gradient
        moved = master - rate * (gradient + DECAY * fresh_velocity)
        moved_list.append(moved)
        velocity_list.append(fresh_velocity)
        average_list.append(0.5 * average + 0.5 * moved)
    return (result, grad_tokens) + tuple(moved_list) + tuple(velocity_list) + tuple(average_list)


def solution(mesh):
    return jax.shard_map(
        local,
        mesh=mesh,
        in_specs=(
            P(("seq", "dp"), None, None),
            P(("seq", "dp"), None),
            P(("seq", "dp"), None),
            P(("seq", "dp"), None, None),
            P("seq", "dp"),
            P("seq", "dp"),
            P("seq", "dp"),
            P("seq", "dp"),
            P("seq", "dp"),
            P("seq", "dp"),
            P("seq", "dp"),
            P("seq", "dp"),
            P("seq", "dp"),
            P("seq", "dp"),
            P("seq", "dp"),
            P("seq", "dp"),
            P("seq", "dp"),
            P("seq", "dp"),
            P("seq", "dp"),
        ),
        out_specs=(
            P(("seq", "dp"), None, None),
            P(("seq", "dp"), None, None),
            P("seq", "dp"),
            P("seq", "dp"),
            P("seq", "dp"),
            P("seq", "dp"),
            P("seq", "dp"),
            P("seq", "dp"),
            P("seq", "dp"),
            P("seq", "dp"),
            P("seq", "dp"),
            P("seq", "dp"),
            P("seq", "dp"),
            P("seq", "dp"),
            P("seq", "dp"),
            P("seq", "dp"),
            P("seq", "dp"),
        ),
        check_vma=False,
    )
```

profile of v0, /device:TPU:0, one launch (start us, length us, event | category | flops | bytes accessed | tf_op | source)
XLA Modules:
  0.0 1213.9 jit_solution(12061338738362880621)
XLA Ops:
  8.6 15.1 %all_gather.40 = bf16[72,6912]{1,0:T(8,128)(2,1)} all-gather(bf16[72,3456]{1,0:T(8,128)(2,1)S(1)} %convert_element_type.148), channel_id=1, replica_groups=mesh['seq'=16,'dp'=2] {'dp'}, dimensions={1}, use_global_device_ids=true | all-gather | bytes 1492992 | tf_op jit(solution)/shard_map/all_gather | solution.py:184
  23.7 8.2 all-gather
  33.6 5.2 all-gather.1
  40.0 7.9 all_gather.46
  49.0 97.9 %all-gather.9.cloned.1.call-done = bf16[1152,6912]{1,0:T(8,128)(2,1)} async-done(((bf16[72,6912]{1,0:T(8,128)(2,1)}), bf16[1152,6912]{1,0:T(8,128)(2,1)}) %all-gather.9.cloned.1.call-update) | async-done | bytes 15925264 | tf_op jit(solution)/shard_map/all_gather | solution.py:189
  146.8 21.6 %copy.55 = bf16[1152,6912]{0,1:T(8,128)(2,1)} copy(bf16[1152,6912]{1,0:T(8,128)(2,1)} %all-gather.9.cloned.1.call-done) | data formatting | bytes 31850496 | tf_op jit(solution)/shard_map/all_gather | solution.py:189
  168.4 9.8 fusion.52
  178.9 41.1 %all-gather.11.cloned.1.call-done = bf16[1152,3456]{1,0:T(8,128)(2,1)} async-done(((bf16[72,3456]{1,0:T(8,128)(2,1)}), bf16[1152,3456]{1,0:T(8,128)(2,1)}) %all-gather.11.cloned.1.call-update) | async-done | bytes 7962640 | tf_op jit(solution)/shard_map/all_gather | solution.py:189
  220.0 7.2 convolution_convert_fusion.4
  234.4 30.1 %all-gather.13.cloned.1.call-done = bf16[1152,1152]{1,0:T(8,128)(2,1)} async-done(((bf16[72,1152]{1,0:T(8,128)(2,1)}), bf16[1152,1152]{1,0:T(8,128)(2,1)}) %all-gather.13.cloned.1.call-update) | async-done | bytes 2654224 | tf_op jit(solution)/shard_map/all_gather | solution.py:189
  270.2 83.8 %all-gather.15.cloned.1.call-done = bf16[1152,4608]{1,0:T(8,128)(2,1)} async-done(((bf16[72,4608]{1,0:T(8,128)(2,1)}), bf16[1152,4608]{1,0:T(8,128)(2,1)}) %all-gather.15.cloned.1.call-update) | async-done | bytes 10616848 | tf_op jit(solution)/shard_map/all_gather | solution.py:189
  354.0 6.6 fusion.63
  362.8 7.3 convolution_convert_fusion
  370.2 118.5 %reduce-scatter.27.cloned.1.call-done = bf16[288,1152]{1,0:T(8,128)(2,1)} async-done(((bf16[4608,1152]{1,0:T(8,128)(2,1)}), bf16[288,1152]{1,0:T(8,128)(2,1)}) %reduce-scatter.27.cloned.1.call-update) | async-done | bytes 663568 | tf_op jit(solution)/shard_map/reduce_scatter | solution.py:302
  491.1 18.6 %reduce-scatter.35.cloned.1.call-done = bf16[576,288]{1,0:T(8,128)(2,1)} async-done(((bf16[1152,288]{1,0:T(8,128)(2,1)}), bf16[576,288]{1,0:T(8,128)(2,1)}) %reduce-scatter.35.cloned.1.call-update) | async-done | bytes 331792
  515.2 11.0 all-gather.2
  530.5 88.8 %all-gather.17.cloned.1.call-done = bf16[4608,1152]{1,0:T(8,128)(2,1)} async-done(((bf16[288,1152]{1,0:T(8,128)(2,1)}), bf16[4608,1152]{1,0:T(8,128)(2,1)}) %all-gather.17.cloned.1.call-update) | async-done | bytes 10616848 | tf_op jit(solution)/shard_map/all_gather | solution.py:189
  619.3 8.6 fusion.6
  627.9 8.8 fusion.20
  637.6 11.0 fusion.19
  666.6 5.7 convolution_convert_fusion.2
  673.6 8.8 convolution_convert_fusion.1
  683.9 6.1 fusion.22
  691.4 5.9 multiply_convert_fusion
  697.4 17.1 %reduce-scatter.41.cloned.1.call-done = bf16[72,1152]{1,0:T(8,128)(2,1)} async-done(((bf16[1152,1152]{1,0:T(8,128)(2,1)}), bf16[72,1152]{1,0:T(8,128)(2,1)}) %reduce-scatter.41.cloned.1.call-update) | async-done | bytes 165904
  716.3 102.5 %reduce-scatter.39.cloned.1.call-done = bf16[72,3456]{1,0:T(8,128)(2,1)} async-done(((bf16[1152,3456]{1,0:T(8,128)(2,1)}), bf16[72,3456]{1,0:T(8,128)(2,1)}) %reduce-scatter.39.cloned.1.call-update) | async-done | bytes 497680
  821.2 121.7 %reduce-scatter.23.cloned.1.call-done = bf16[72,4608]{1,0:T(8,128)(2,1)} async-done(((bf16[1152,4608]{1,0:T(8,128)(2,1)}), bf16[72,4608]{1,0:T(8,128)(2,1)}) %reduce-scatter.23.cloned.1.call-update) | async-done | bytes 663568 | tf_op jit(solution)/shard_map/reduce_scatter | solution.py:299
  944.0 174.6 %reduce-scatter.29.cloned.1.call-done = bf16[72,6912]{1,0:T(8,128)(2,1)} async-done(((bf16[1152,6912]{1,0:T(8,128)(2,1)}), bf16[72,6912]{1,0:T(8,128)(2,1)}) %reduce-scatter.29.cloned.1.call-update) | async-done | bytes 995344 | tf_op jit(solution)/shard_map/reduce_scatter | solution.py:305
  1123.5 9.0 reduce-scatter.33.cloned.1.call-done
  1135.5 18.4 %reduce-scatter.31.cloned.1.call-done = bf16[1728,72]{1,0:T(8,128)(2,1)} async-done(((bf16[3456,72]{1,0:T(8,128)(2,1)}), bf16[1728,72]{1,0:T(8,128)(2,1)}) %reduce-scatter.31.cloned.1.call-update) | async-done | bytes 248848
  1156.4 15.7 %reduce-scatter.25.cloned.1.call-done = bf16[72,2304]{1,0:T(8,128)(2,1)} async-done(((bf16[72,4608]{1,0:T(8,128)(2,1)}), bf16[72,2304]{1,0:T(8,128)(2,1)}) %reduce-scatter.25.cloned.1.call-update) | async-done | bytes 331792 | tf_op jit(solution)/shard_map/reduce_scatter | solution.py:316
  1174.8 27.7 %reduce-scatter.37.cloned.1.call-done = bf16[3456,72]{1,0:T(8,128)(2,1)} async-done(((bf16[6912,72]{1,0:T(8,128)(2,1)}), bf16[3456,72]{1,0:T(8,128)(2,1)}) %reduce-scatter.37.cloned.1.call-update) | async-done | bytes 497680
  (216 shorter events, 78.8 us)
Async XLA Ops:
  7.2 16.5 %copy-start.16 = (f32[72,1728]{1,0:T(8,128)S(1)}, f32[72,1728]{1,0:T(8,128)}, u32[]{:S(2)}) copy-start(f32[72,1728]{1,0:T(8,128)} %param.23) | copy-start | bytes 1492996
  7.2 139.6 %all-gather.9.cloned.1.call-start = ((), (), s32[]{:S(2)}) async-start(), calls=%async_computation.10 | async-start | bytes 16920576 | tf_op jit(solution)/shard_map/all_gather | solution.py:189
  23.6 196.4 %all-gather.11.cloned.1.call-start = ((), (), s32[]{:S(2)}) async-start(), calls=%async_computation.11 | async-start | bytes 8460288 | tf_op jit(solution)/shard_map/all_gather | solution.py:189
  33.5 230.9 %all-gather.13.cloned.1.call-start = ((), (), s32[]{:S(2)}) async-start(), calls=%async_computation.12 | async-start | bytes 2820096 | tf_op jit(solution)/shard_map/all_gather | solution.py:189
  39.9 314.1 %all-gather.15.cloned.1.call-start = ((), (), s32[]{:S(2)}) async-start(), calls=%async_computation.13 | async-start | bytes 11280384 | tf_op jit(solution)/shard_map/all_gather | solution.py:189
  47.9 440.8 %reduce-scatter.27.cloned.1.call-start = ((), (), s32[]{:S(2)}) async-start(), calls=%async_computation.17 | async-start | bytes 11280384 | tf_op jit(solution)/shard_map/reduce_scatter | solution.py:302
  48.7 171.3 %copy-start.37 = (f32[256]{0:T(256)}, f32[256]{0:T(256)S(1)}, u32[]{:S(2)}) copy-start(f32[256]{0:T(256)S(1)} %broadcast_multiply_fusion.5) | copy-start | bytes 3076
  48.9 171.0 %copy-start.45 = (f32[256]{0:T(256)}, f32[256]{0:T(256)S(1)}, u32[]{:S(2)}) copy-start(f32[256]{0:T(256)S(1)} %add_rsqrt_fusion.1) | copy-start | bytes 3076
  49.0 119.5 %copy-start.39 = (f32[1,1152]{1,0:T(1,128)S(1)}, f32[1,1152]{1,0:T(1,128)}, u32[]{:S(2)}) copy-start(f32[1,1152]{1,0:T(1,128)} %param.20) | copy-start | bytes 13828
  178.9 41.1 %copy-start.24 = (f32[1152]{0:T(1024)}, f32[1152]{0:T(1024)S(1)}, u32[]{:S(2)}) copy-start(f32[1152]{0:T(1024)S(1)} %get-tuple-element.73) | copy-start | bytes 13828
  178.9 41.1 %copy-start.30 = (f32[1152]{0:T(1024)}, f32[1152]{0:T(1024)S(1)}, u32[]{:S(2)}) copy-start(f32[1152]{0:T(1024)S(1)} %get-tuple-element.72) | copy-start | bytes 13828
  178.9 458.6 %copy-start.28 = (f32[1152]{0:T(1024)}, f32[1152]{0:T(1024)S(1)}, u32[]{:S(2)}) copy-start(f32[1152]{0:T(1024)S(1)} %get-tuple-element.71) | copy-start | bytes 13828
  178.9 469.7 %copy-start.32 = (f32[1152]{0:T(1024)}, f32[1152]{0:T(1024)S(1)}, u32[]{:S(2)}) copy-start(f32[1152]{0:T(1024)S(1)} %get-tuple-element.74) | copy-start | bytes 13828
  370.1 139.5 %reduce-scatter.35.cloned.1.call-start = ((), (), s32[]{:S(2)}) async-start(), calls=%async_computation.21 | async-start | bytes 1327104
  491.0 128.3 %all-gather.17.cloned.1.call-start = ((), (), s32[]{:S(2)}) async-start(), calls=%async_computation.14 | async-start | bytes 11280384 | tf_op jit(solution)/shard_map/all_gather | solution.py:189
  530.4 184.0 %reduce-scatter.41.cloned.1.call-start = ((), (), s32[]{:S(2)}) async-start(), calls=%async_computation.24 | async-start | bytes 2820096
  652.2 166.6 %reduce-scatter.39.cloned.1.call-start = ((), (), s32[]{:S(2)}) async-start(), calls=%async_computation.23 | async-start | bytes 8460288
  672.4 270.5 %reduce-scatter.23.cloned.1.call-start = ((), (), s32[]{:S(2)}) async-start(), calls=%async_computation.15 | async-start | bytes 11280384 | tf_op jit(solution)/shard_map/reduce_scatter | solution.py:299
  682.4 436.3 %reduce-scatter.29.cloned.1.call-start = ((), (), s32[]{:S(2)}) async-start(), calls=%async_computation.18 | async-start | bytes 16920576 | tf_op jit(solution)/shard_map/reduce_scatter | solution.py:305
  697.3 435.2 %reduce-scatter.33.cloned.1.call-start = ((), (), s32[]{:S(2)}) async-start(), calls=%async_computation.20 | async-start | bytes 442368
  716.3 437.6 %reduce-scatter.31.cloned.1.call-start = ((), (), s32[]{:S(2)}) async-start(), calls=%async_computation.19 | async-start | bytes 1327104
  821.1 351.0 %reduce-scatter.25.cloned.1.call-start = ((), (), s32[]{:S(2)}) async-start(), calls=%async_computation.16 | async-start | bytes 995328 | tf_op jit(solution)/shard_map/reduce_scatter | solution.py:316
  942.9 259.7 %reduce-scatter.37.cloned.1.call-start = ((), (), s32[]{:S(2)}) async-start(), calls=%async_computation.22 | async-start | bytes 2654208
  944.0 177.3 %copy-start.9 = (f32[1,256,1152]{2,1,0:T(8,128)S(1)}, f32[1,256,1152]{2,1,0:T(8,128)}, u32[]{:S(2)}) copy-start(f32[1,256,1152]{2,1,0:T(8,128)} %copy-done.8) | copy-start | bytes 3538948
  944.0 177.3 %copy-start.11 = (f32[256,1152]{1,0:T(8,128)S(1)}, f32[256,1152]{1,0:T(8,128)}, u32[]{:S(2)}) copy-start(f32[256,1152]{1,0:T(8,128)} %copy-done.10) | copy-start | bytes 3538948
  1123.5 31.6 %copy-start.17 = (f32[72,1728]{1,0:T(8,128)S(1)}, f32[72,1728]{1,0:T(8,128)}, u32[]{:S(2)}) copy-start(f32[72,1728]{1,0:T(8,128)} %param.23) | copy-start | bytes 1492996
  1123.5 31.6 %copy-start.22 = (f32[72,1728]{1,0:T(8,128)S(1)}, f32[72,1728]{1,0:T(8,128)}, u32[]{:S(2)}) copy-start(f32[72,1728]{1,0:T(8,128)} %param.33) | copy-start | bytes 1492996
  1123.5 31.6 %copy-start.23 = (f32[72,1728]{1,0:T(8,128)S(1)}, f32[72,1728]{1,0:T(8,128)}, u32[]{:S(2)}) copy-start(f32[72,1728]{1,0:T(8,128)} %param.28) | copy-start | bytes 1492996
  1155.1 17.0 %copy-start.14 = (f32[72,2304]{1,0:T(8,128)S(1)}, f32[72,2304]{1,0:T(8,128)}, u32[]{:S(2)}) copy-start(f32[72,2304]{1,0:T(8,128)} %param.25) | copy-start | bytes 1990660
  1155.1 17.0 %copy-start.21 = (f32[72,2304]{1,0:T(8,128)S(1)}, f32[72,2304]{1,0:T(8,128)}, u32[]{:S(2)}) copy-start(f32[72,2304]{1,0:T(8,128)} %param.35) | copy-start | bytes 1990660
  1172.1 32.0 %copy-start.19 = (f32[72,3456]{1,0:T(8,128)S(1)}, f32[72,3456]{1,0:T(8,128)}, u32[]{:S(2)}) copy-start(f32[72,3456]{1,0:T(8,128)} %param.37) | copy-start | bytes 2985988
  1174.8 29.3 %copy-start.12 = (f32[72,3456]{1,0:T(8,128)S(1)}, f32[72,3456]{1,0:T(8,128)}, u32[]{:S(2)}) copy-start(f32[72,3456]{1,0:T(8,128)} %param.27) | copy-start | bytes 2985988
  (44 other events, 199.2 us)
Sparse Core Ops, SparseCore 0:
  23.8 123.0 all-gather.8
  149.6 70.3 all-gather.10
  222.7 41.6 all-gather.12
  266.6 87.3 all-gather.14
  370.3 118.3 reduce-scatter.26
  491.4 18.2 reduce-scatter.34
  530.5 88.6 all-gather.16
  652.4 62.0 reduce-scatter.40
  719.1 99.7 reduce-scatter.38
  822.7 120.0 reduce-scatter.22
  947.0 171.6 reduce-scatter.28
  1121.3 11.1 reduce-scatter.32
  1135.3 18.4 reduce-scatter.30
  1156.0 16.0 reduce-scatter.24
  1174.3 28.2 reduce-scatter.36
where the time goes:
time: 1220 us; the launch traced here: 1210 us
  waiting for transfers between devices  966 us (79%)
  matrix products  97.9 us (8%)
  local copies, waits for them, and re-layouts  58.7 us (5%)
  blocking collectives  47.4 us (4%)
  other arithmetic  28.3 us (2%)
  between operations  14.8 us (1%)
    all_gather x5, waiting for transfers between devices, local(): lax.all_gather(for_sending(widened), 'seq', axis=0, tiled=True)  342 us
    unnamed x21, waiting for transfers between devices  194 us
    reduce_scatter x1, waiting for transfers between devices, local(): lax.psum_scatter(grad_modulate.astype(jnp.bfloat16), 'seq', scatter_dimen...  175 us
    reduce_scatter x1, waiting for transfers between devices, local(): lax.psum_scatter(grad_expand.astype(jnp.bfloat16), 'seq', scatter_dimensi...  122 us
    reduce_scatter x1, waiting for transfers between devices, local(): lax.psum_scatter(grad_shrink.astype(jnp.bfloat16), 'seq', scatter_dimensi...  118 us
    all_gather x5, blocking collectives, local(): lax.all_gather(for_sending(halves), 'dp', axis=1, tiled=True)  47.4 us
    unnamed x133, local copies, waits for them, and re-layouts  31.1 us
  transfers between devices with their start and end apart: 15, of which 15 were waited for; matrix products, arithmetic and copies ran while one was open for 9% of the time, Pallas kernels for 0%

commit v1 on v0

v1 whole, which is shorter than its diff:
```python
import math

import jax
import jax.numpy as jnp
from jax import lax
from jax.experimental import pallas as pl
from jax.experimental.pallas import tpu as pltpu
from jax.sharding import PartitionSpec as P

HEADS = 16
EPSILON = 1e-06
DECAY = 0.5
BF = jnp.bfloat16
F32 = jnp.float32


def normalize(values):
    average = jnp.mean(values, axis=-1, keepdims=True)
    centred = values - average
    inverse = lax.rsqrt(jnp.mean(centred * centred, axis=-1, keepdims=True) + EPSILON)
    return (centred * inverse, inverse)


def norm_back(gradient, normed, inverse):
    return inverse * (
        gradient
        - jnp.mean(gradient, axis=-1, keepdims=True)
        - normed * jnp.mean(gradient * normed, axis=-1, keepdims=True)
    )


def place_kernel(count, depth, order, *refs):
    blocks, out, sems = refs[:count], refs[count], refs[count + 1]
    copies = []
    for b in range(count):
        for i in range(depth):
            at = b * depth + i
            copies.append(pltpu.make_async_copy(blocks[b].at[i], out.at[order[at]], sems.at[at]))
    for copy in copies:
        copy.start()
    for copy in copies:
        copy.wait()


def pick_kernel(count, depth, order, whole, *refs):
    blocks, sems = refs[:count], refs[count]
    copies = []
    for b in range(count):
        for i in range(depth):
            at = b * depth + i
            copies.append(pltpu.make_async_copy(whole.at[order[at]], blocks[b].at[i], sems.at[at]))
    for copy in copies:
        copy.start()
    for copy in copies:
        copy.wait()


def place(blocks, order):
    count, (depth, rows, columns) = len(blocks), blocks[0].shape
    total = count * depth
    return pl.pallas_call(
        lambda *refs: place_kernel(count, depth, *refs),
        out_shape=jax.ShapeDtypeStruct((total, rows, columns), blocks[0].dtype),
        in_specs=[pl.BlockSpec(memory_space=pltpu.SMEM)] + [pl.BlockSpec(memory_space=pl.ANY)] * count,
        out_specs=pl.BlockSpec(memory_space=pltpu.VMEM),
        scratch_shapes=[pltpu.SemaphoreType.DMA((total,))],
        compiler_params=pltpu.CompilerParams(vmem_limit_bytes=48 * 2**20),
        cost_estimate=pl.CostEstimate(
            flops=0, bytes_accessed=4 * total * rows * columns, transcendentals=0
        ),
        name="place",
    )(order, *blocks)


def pick(whole, order, count):
    total, rows, columns = whole.shape
    depth = total // count
    return pl.pallas_call(
        lambda *refs: pick_kernel(count, depth, *refs),
        out_shape=[jax.ShapeDtypeStruct((depth, rows, columns), whole.dtype)] * count,
        in_specs=[pl.BlockSpec(memory_space=pltpu.SMEM), pl.BlockSpec(memory_space=pltpu.VMEM)],
        out_specs=[pl.BlockSpec(memory_space=pl.ANY)] * count,
        scratch_shapes=[pltpu.SemaphoreType.DMA((total,))],
        compiler_params=pltpu.CompilerParams(vmem_limit_bytes=48 * 2**20),
        cost_estimate=pl.CostEstimate(
            flops=0, bytes_accessed=4 * total * rows * columns, transcendentals=0
        ),
        name="pick",
    )(order, whole)


class Grid:
    def __init__(self, seq, dp):
        self.size = {"z": 4, "y": seq // 8, "c": 2, "x": dp}
        assert seq % 8 == 0
        at, column = lax.axis_index("seq"), lax.axis_index("dp")
        sizes = self.size
        self.at = {
            "z": at // (2 * sizes["y"]),
            "y": (at // 2) % sizes["y"],
            "c": at % 2,
            "x": column,
        }

    def send(self, value, axis, shift):
        sizes = self.size
        pairs = []
        for z in range(sizes["z"]):
            for y in range(sizes["y"]):
                for c in range(2):
                    for x in range(sizes["x"]):
                        here = {"z": z, "y": y, "c": c, "x": x}
                        there = dict(here)
                        there[axis] = (here[axis] + shift) % sizes[axis]
                        pairs.append((self.flat(here), self.flat(there)))
        return lax.ppermute(value, ("seq", "dp"), pairs)

    def flat(self, p):
        sizes = self.size
        return ((p["z"] * sizes["y"] + p["y"]) * 2 + p["c"]) * sizes["x"] + p["x"]

    def swap(self, value):
        return self.send(value, "c", 1)

    def off(self, axis, shift):
        return (self.at[axis] + shift) % self.size[axis]


def gather_small(grid, value, axes):
    for axis in axes:
        value = jnp.stack(
            [value] + [grid.send(value, axis, shift) for shift in range(1, grid.size[axis])]
        )
    return value


def to_order(grid, values, axis):
    count = len(values)
    line = jnp.stack(values + values[:-1])
    return lax.dynamic_slice_in_dim(line, (count - grid.at[axis]) % count, count, axis=0)


def gather_part(grid, piece, last):
    sizes = grid.size
    stack = jnp.stack([piece] + [grid.send(piece, "z", shift) for shift in range(1, sizes["z"])])
    if sizes["x"] > 2:
        line = [stack] + [grid.send(stack, "y", shift) for shift in range(1, sizes["y"])]
        whole = lax.all_gather(jnp.stack(line), "dp", axis=0)
        return [whole[x, sy] for x in range(sizes["x"]) for sy in range(sizes["y"])]
    first = "y" if last == "x" else "x"
    blocks = {(0, 0): stack}
    for shift in range(1, sizes[first]):
        blocks[(shift, 0)] = grid.send(stack, first, shift)
    for shift in range(sizes[first]):
        for far in range(1, sizes[last]):
            blocks[(shift, far)] = grid.send(blocks[(shift, 0)], last, far)
    if first == "x":
        return [blocks[(sx, sy)] for sx in range(sizes["x"]) for sy in range(sizes["y"])]
    return [blocks[(sy, sx)] for sx in range(sizes["x"]) for sy in range(sizes["y"])]


def scatter_part(grid, blocks, last):
    sizes = grid.size
    if sizes["x"] > 2:
        pairs = jnp.stack(blocks).reshape((sizes["x"], sizes["y"]) + blocks[0].shape)
        kept = lax.psum_scatter(pairs, "dp", scatter_dimension=0).astype(F32)
        return scatter_line(grid, [kept[sy] for sy in range(sizes["y"])], "y")
    at = {}
    it = iter(blocks)
    for sx in range(sizes["x"]):
        for sy in range(sizes["y"]):
            at[(sx, sy) if last == "y" else (sy, sx)] = next(it)
    first = "y" if last == "x" else "x"
    kept = []
    for near in range(sizes[first] - 1, -1, -1):
        total = at[(near, 0)].astype(F32)
        for far in range(1, sizes[last]):
            total = total + grid.send(at[(near, far)], last, far).astype(F32)
        kept.append(total)
    return scatter_line(grid, kept[::-1], first)


def scatter_line(grid, kept, axis):
    sizes = grid.size
    total = kept[0]
    for near in range(1, sizes[axis]):
        total = total + grid.send(kept[near].astype(BF), axis, near).astype(F32)
    result = total[0]
    for shift in range(1, sizes["z"]):
        result = result + grid.send(total[shift].astype(BF), "z", shift).astype(F32)
    return result


def orders(grid, sign, parts):
    sizes = grid.size
    result = []
    for part in parts:
        for sx in range(sizes["x"]):
            for sy in range(sizes["y"]):
                for sz in range(sizes["z"]):
                    x = grid.off("x", sign * sx) if sizes["x"] == 2 else sx
                    y = grid.off("y", sign * sy)
                    z = grid.off("z", sign * sz)
                    result.append(((x * sizes["z"] + z) * sizes["y"] + y) * len(parts) + part)
    return jnp.stack(result).astype(jnp.int32)


def gather(grid, pieces, lasts, parts):
    blocks = []
    for piece, last in zip(pieces, lasts):
        blocks += gather_part(grid, piece, last)
    rows, columns = pieces[0].shape
    whole = place(blocks, orders(grid, -1, parts))
    return whole.reshape(grid.size["x"], -1, columns)


def scatter(grid, whole, rows, lasts, parts):
    columns = whole.shape[-1]
    sizes = grid.size
    count = len(parts) * sizes["x"] * sizes["y"]
    blocks = pick(whole.astype(BF).reshape(-1, rows, columns), orders(grid, 1, parts), count)
    each = count // len(parts)
    return [
        scatter_part(grid, blocks[i * each : (i + 1) * each], last) for i, last in enumerate(lasts)
    ]


def heads_of(grid, whole, rows, head_size):
    if rows % head_size == 0:
        return whole
    assert head_size == 2 * rows
    first = grid.at["c"] == 0
    halves = whole.reshape(whole.shape[0], HEADS // 2, 2, rows, -1)
    even, odd = halves[:, :, 0], halves[:, :, 1]
    kept = jnp.where(first, even, odd)
    came = grid.swap(jnp.where(first, odd, even))
    low, high = jnp.where(first, kept, came), jnp.where(first, came, kept)
    return jnp.stack([low, high], axis=2).reshape(whole.shape)


def rows_of(grid, whole, rows, head_size):
    if rows % head_size == 0:
        return whole
    first = grid.at["c"] == 0
    halves = whole.reshape(whole.shape[0], HEADS // 2, 2, rows, -1)
    low, high = halves[:, :, 0], halves[:, :, 1]
    kept = jnp.where(first, low, high)
    came = grid.swap(jnp.where(first, high, low))
    even, odd = jnp.where(first, kept, came), jnp.where(first, came, kept)
    return jnp.stack([even, odd], axis=2).reshape(whole.shape)


def split_core(grid, weight, block):
    rows, columns = weight.shape
    pairs = weight.reshape(rows, columns // (2 * block), 2, block)
    even = pairs[:, :, 0].reshape(rows, -1)
    odd = pairs[:, :, 1].reshape(rows, -1)
    first = grid.at["c"] == 0
    return (jnp.where(first, even, odd), jnp.where(first, odd, even))


def join_core(grid, own, other, block):
    rows, columns = own.shape
    first = grid.at["c"] == 0
    even = jnp.where(first, own, other).reshape(rows, -1, 1, block)
    odd = jnp.where(first, other, own).reshape(rows, -1, 1, block)
    return jnp.concatenate([even, odd], axis=2).reshape(rows, 2 * columns)


def attend(projected, kept):
    group, length, triple = projected.shape
    width = triple // 3
    head_size = width // (HEADS // 2)
    sections = projected.reshape(group, length, 3, HEADS // 2, head_size)
    queries, keys_part, values = sections[:, :, 0], sections[:, :, 1], sections[:, :, 2]
    scale = 1.0 / math.sqrt(head_size)
    scores = (
        jnp.einsum("gqhd,gkhd->ghqk", queries, keys_part, preferred_element_type=F32) * scale
    )
    scores = jnp.where(kept[:, None, None, :] > 0, scores, -1000000000.0)
    row_max = jnp.max(scores, axis=-1, keepdims=True)
    exponent = jnp.exp(scores - row_max)
    soft = exponent / jnp.sum(exponent, axis=-1, keepdims=True)
    attended = jnp.einsum("ghqk,gkhd->gqhd", soft.astype(BF), values, preferred_element_type=F32)
    return (attended.astype(BF).reshape(group * length, width), soft)


def attend_back(projected, soft, grad_attended):
    group, length, triple = projected.shape
    width = triple // 3
    head_size = width // (HEADS // 2)
    sections = projected.reshape(group, length, 3, HEADS // 2, head_size)
    queries, keys_part, values = sections[:, :, 0], sections[:, :, 1], sections[:, :, 2]
    scale = 1.0 / math.sqrt(head_size)
    upstream = grad_attended.reshape(group, length, HEADS // 2, head_size)
    grad_soft = jnp.einsum("gqhd,gkhd->ghqk", upstream, values, preferred_element_type=F32)
    grad_scores = (soft * (grad_soft - jnp.sum(soft * grad_soft, axis=-1, keepdims=True))).astype(BF)
    grad_queries = (
        jnp.einsum("ghqk,gkhd->gqhd", grad_scores, keys_part, preferred_element_type=F32) * scale
    )
    grad_keys = (
        jnp.einsum("ghqk,gqhd->gkhd", grad_scores, queries, preferred_element_type=F32) * scale
    )
    grad_values = jnp.einsum(
        "ghqk,gqhd->gkhd", soft.astype(BF), upstream, preferred_element_type=F32
    )
    stacked = jnp.stack([grad_queries, grad_keys, grad_values], axis=2).astype(BF)
    return stacked.reshape(group * length, triple)


def times(rows, weight):
    out = jnp.einsum("tr,xrk->txk", rows, weight, preferred_element_type=F32)
    return out.reshape(out.shape[0], -1)


def times_back(grads, weight):
    split = grads.reshape(grads.shape[0], weight.shape[0], weight.shape[2])
    return jnp.einsum("txk,xrk->tr", split, weight, preferred_element_type=F32)


def outer(rows, grads, count):
    split = grads.reshape(grads.shape[0], count, -1)
    return jnp.einsum("tr,txk->xrk", rows, split, preferred_element_type=F32).astype(BF)


def local(seq, dp, *arguments):
    tokens, condition, kept_tokens, grad_out = arguments[:4]
    masters, velocities, averages = arguments[4:9], arguments[9:14], arguments[14:19]
    entry_own, merge_own, expand_own, shrink_own, modulate_own = [
        master.astype(BF) for master in masters
    ]
    grid = Grid(seq, dp)
    latents, length, width = tokens.shape
    head_size = width // HEADS
    both = 2 * latents
    rows = latents * length
    core = grid.at["c"]
    x_count = grid.size["x"]

    lifted = jax.nn.silu(condition).astype(BF)
    every_lifted = gather_small(grid, lifted, "xcyz")
    part_rows = modulate_own.shape[0]
    my_lifted = lax.dynamic_slice_in_dim(
        every_lifted, lax.axis_index("seq") * part_rows, part_rows, axis=-1
    )
    partial = jnp.einsum("zycxlr,re->zycxle", my_lifted, modulate_own, preferred_element_type=F32)
    for axis in "zyc":
        total = partial[0]
        for shift in range(1, grid.size[axis]):
            total = total + grid.send(partial[shift], axis, -shift)
        partial = total
    mine = [partial[0]] + [grid.send(partial[shift], "x", -shift) for shift in range(1, dp)]
    table = to_order(grid, mine, "x")
    table = jnp.moveaxis(table, 0, 1).reshape(latents, 6, width)
    shift_one, scale_one, gate_one, shift_two, scale_two, gate_two = [
        table[:, number][:, None, :] for number in range(6)
    ]

    ff_block = shrink_own.shape[0]
    entry_mine, entry_theirs = split_core(grid, entry_own, head_size)
    expand_mine, expand_theirs = split_core(grid, expand_own, ff_block)
    entry_other = grid.swap(entry_theirs)
    expand_other = grid.swap(expand_theirs)
    core_parts = (core, 1 - core)
    half = ff_block // 2
    entry = gather(grid, (entry_mine, entry_other), "xy", core_parts)
    merge = heads_of(grid, gather(grid, (merge_own,), "x", (0,)), part_rows, head_size)
    expand = gather(grid, (expand_mine, expand_other), "xy", core_parts)
    shrink = gather(grid, (shrink_own[:half], shrink_own[half:]), "xy", (0, 1))

    kept_mask = kept_tokens.astype(F32)
    kept_both = jnp.concatenate([kept_mask, grid.swap(kept_mask)])
    kept_mask = kept_mask[:, :, None]

    def share(value):
        flat = value.reshape(rows, -1)
        return jnp.concatenate([flat, grid.swap(flat)])

    def settle(value):
        return (value[:rows] + grid.swap(value[rows:])).reshape(latents, length, -1)

    grad_feed = share((kept_mask * gate_two * grad_out).astype(BF))
    normed_one, inverse_one = normalize(tokens)
    hidden_one = share((normed_one * (1.0 + scale_one) + shift_one).astype(BF))
    projected = times(hidden_one, entry).astype(BF).reshape(both, length, -1)
    attended, soft = attend(projected, kept_both)
    attention_out = settle(times(attended, merge))
    middle = tokens + kept_mask * gate_one * attention_out
    normed_two, inverse_two = normalize(middle)
    hidden_two = share((normed_two * (1.0 + scale_two) + shift_two).astype(BF))
    expanded = times(hidden_two, expand)
    activated = jax.nn.gelu(expanded).astype(BF)
    feed = settle(times(activated, shrink))
    result = middle + kept_mask * gate_two * feed

    grad_gate_two = jnp.sum(kept_mask * feed * grad_out, axis=1)
    grad_shrink = outer(activated, grad_feed, x_count)
    shrink_sums = scatter(grid, grad_shrink, half, "xy", (0, 1))
    grad_activated = times_back(grad_feed, shrink)
    grad_expanded = jax.vjp(jax.nn.gelu, expanded)[1](grad_activated)[0].astype(BF)
    grad_expand = outer(hidden_two, grad_expanded, x_count)
    expand_sums = scatter(grid, grad_expand, part_rows, "xy", core_parts)
    grad_hidden_two = settle(times_back(grad_expanded, expand))
    grad_scale_two = jnp.sum(grad_hidden_two * normed_two, axis=1)
    grad_shift_two = jnp.sum(grad_hidden_two, axis=1)
    grad_middle = grad_out + norm_back(grad_hidden_two * (1.0 + scale_two), normed_two, inverse_two)
    grad_attention = share((kept_mask * gate_one * grad_middle).astype(BF))
    grad_gate_one = jnp.sum(kept_mask * attention_out * grad_middle, axis=1)
    grad_merge = outer(attended, grad_attention, x_count)
    grad_merge = rows_of(grid, grad_merge, part_rows, head_size)
    merge_sums = scatter(grid, grad_merge, part_rows, "x", (0,))
    grad_attended = times_back(grad_attention, merge).astype(BF)
    grad_projected = attend_back(projected, soft, grad_attended)
    grad_entry = outer(hidden_one, grad_projected, x_count)
    entry_sums = scatter(grid, grad_entry, part_rows, "xy", core_parts)
    grad_hidden_one = settle(times_back(grad_projected, entry))
    grad_scale_one = jnp.sum(grad_hidden_one * normed_one, axis=1)
    grad_shift_one = jnp.sum(grad_hidden_one, axis=1)
    grad_tokens = grad_middle + norm_back(
        grad_hidden_one * (1.0 + scale_one), normed_one, inverse_one
    )
    grad_table = jnp.concatenate(
        [
            grad_shift_one,
            grad_scale_one,
            grad_gate_one,
            grad_shift_two,
            grad_scale_two,
            grad_gate_two,
        ],
        axis=1,
    ).astype(BF)
    columns = modulate_own.shape[1]
    away = [
        lax.dynamic_slice_in_dim(grad_table, grid.off("x", shift) * columns, columns, axis=1)
        for shift in range(dp)
    ]
    for_me = jnp.stack(
        [away[0]] + [grid.send(away[shift], "x", shift) for shift in range(1, dp)]
    )
    every_table = gather_small(grid, for_me, "cyz")
    modulate_sum = jnp.einsum(
        "zycxlr,zycxle->re", my_lifted, every_table, preferred_element_type=F32
    )

    entry_sum = join_core(grid, entry_sums[0], grid.swap(entry_sums[1]), head_size)
    expand_sum = join_core(grid, expand_sums[0], grid.swap(expand_sums[1]), ff_block)
    shrink_sum = jnp.concatenate(shrink_sums)
    summed = (entry_sum, merge_sums[0], expand_sum, shrink_sum, modulate_sum)

    rate = 0.03 / math.sqrt(rows * seq * dp)
    moved_list = []
    velocity_list = []
    average_list = []
    for master, velocity, average, gradient in zip(masters, velocities, averages, summed):
        fresh_velocity = DECAY * velocity + gradient
        moved = master - rate * (gradient + DECAY * fresh_velocity)
        moved_list.append(moved)
        velocity_list.append(fresh_velocity)
        average_list.append(0.5 * average + 0.5 * moved)
    return (result, grad_tokens) + tuple(moved_list) + tuple(velocity_list) + tuple(average_list)


def solution(mesh):
    spread = P(("seq", "dp"), None, None)
    flat = P(("seq", "dp"), None)
    weight = P("seq", "dp")
    seq, dp = mesh.shape["seq"], mesh.shape["dp"]
    return jax.shard_map(
        lambda *arguments: local(seq, dp, *arguments),
        mesh=mesh,
        in_specs=(spread, flat, flat, spread) + (weight,) * 15,
        out_specs=(spread, spread) + (weight,) * 15,
        check_vma=False,
    )
```

time: 1220 us -> 685 us (0.56)
  waiting for transfers between devices: 966 us -> 256 us
  starting transfers between devices: 1 us -> 138 us
  Pallas kernels: 0 us -> 54.2 us
  blocking collectives: 47.4 us -> 0 us
  local copies, waits for them, and re-layouts: 58.7 us -> 93.5 us
  other arithmetic: 28.3 us -> 59.3 us
  matrix products: 97.9 us -> 70.8 us
    reduce_scatter x4 -> x0, waiting for transfers between devices: 431 us -> none  [the longest x1 175 us: local(): lax.psum_scatter(grad_modulate.astype(jnp.bfloat16), 'seq', scatter_dimen...]
    all_gather x5 -> x0, waiting for transfers between devices: 342 us -> none  [local(): lax.all_gather(for_sending(widened), 'seq', axis=0, tiled=True)]
    ppermute x0 -> x115, waiting for transfers between devices: none -> 256 us  [send(): return lax.ppermute(value, ('seq', 'dp'), pairs)]
    unnamed x21 -> x0, waiting for transfers between devices: 194 us -> none
    ppermute x0 -> x115, starting transfers between devices: none -> 138 us  [send(): return lax.ppermute(value, ('seq', 'dp'), pairs)]
    pallas_call x0 -> x8, Pallas kernels: none -> 54.2 us  [the longest x4 31.2 us: pick(): pl.pallas_call(lambda *refs: pick_kernel(count, depth, *refs), out_shape=...]
    all_gather x5 -> x0, blocking collectives: 47.4 us -> none  [local(): lax.all_gather(for_sending(halves), 'dp', axis=1, tiled=True)]
    reshape x0 -> x12, local copies, waits for them, and re-layouts: none -> 28.2 us  [the longest x2 15 us: gather(): return whole.reshape(grid.size['x'], -1, columns)]
  transfers between devices with their start and end apart: 15 -> 115, of which waited for: 15 -> 50; matrix products, arithmetic and copies ran while one was open for 9% -> 24% of each run, Pallas kernels for 0% -> 4%
where the time goes in v1:
time: 685 us; the launch traced here: 675 us
  waiting for transfers between devices  256 us (37%)
  starting transfers between devices  138 us (20%)
  local copies, waits for them, and re-layouts  93.5 us (14%)
  matrix products  70.8 us (10%)
  other arithmetic  59.3 us (9%)
  Pallas kernels  54.2 us (8%)
    ppermute x115, waiting for transfers between devices, send(): return lax.ppermute(value, ('seq', 'dp'), pairs)  256 us
    ppermute x115, starting transfers between devices, send(): return lax.ppermute(value, ('seq', 'dp'), pairs)  138 us
    pallas_call x4, Pallas kernels, pick(): pl.pallas_call(lambda *refs: pick_kernel(count, depth, *refs), out_shape=...  31.2 us
    pallas_call x4, Pallas kernels, place(): pl.pallas_call(lambda *refs: place_kernel(count, depth, *refs), out_shape...  23 us
    dot_general x4, matrix products, times_back(): return jnp.einsum('txk,xrk->tr', split, weight, preferred_element_type=F32)  22 us
    dot_general x4, matrix products, times(): out = jnp.einsum('tr,xrk->txk', rows, weight, preferred_element_type=F32)  21.2 us
    dot_general x4, matrix products, outer(): jnp.einsum('tr,txk->xrk', rows, split, preferred_element_type=F32)  18.2 us
    reshape x2, local copies, waits for them, and re-layouts, gather(): return whole.reshape(grid.size['x'], -1, columns)  15 us
  transfers between devices with their start and end apart: 115, of which 50 were waited for; matrix products, arithmetic and copies ran while one was open for 24% of the time, Pallas kernels for 4%

profile of v1, /device:TPU:0, one launch (start us, length us, event | category | flops | bytes accessed | tf_op | source)
XLA Modules:
  0.0 674.5 jit_solution(5978466853083814052)
XLA Ops:
  46.6 7.3 %collective-permute-start.13 = (bf16[72,864]{1,0:T(8,128)(2,1)S(1)}, bf16[72,864]{1,0:T(8,128)(2,1)S(1)}, u32[]{:S(2)}, u32[]{:S(2)}) collective-permute-start(bf16[72,864]{1,0:T(8,128)(2,1)S(1)} %select_n.1510), channel_id=1, source_target_pairs={{0,8},{1,9},{2,10},{3,11},{4,12},{5,13},{6,14},{7,15},{8,16},{9,17... | collective-permute-start | bytes 373256 | tf_op jit(solution)/shard_map/ppermute | solution.py:116
  80.8 13.7 %collective-permute-done.32.refs_4_ = bf16[4,72,576]{2,1,0:T(8,128)(2,1)S(1)} collective-permute-done((bf16[4,72,576]{2,1,0:T(8,128)(2,1)S(1)}, bf16[4,72,576]{2,1,0:T(8,128)(2,1)S(1)}, u32[]{:S(2)}, u32[]{:S(2)}) %collective-permute-start.32) | collective-permute-done | bytes 331808 | tf_op jit(solution)/shard_map/ppermute | solution.py:116
  118.6 6.5 place.4
  125.1 6.5 copy.226
  131.6 6.3 convolution_convert_fusion.3
  161.3 10.0 %collective-permute-done.43 = bf16[72,1152]{1,0:T(8,128)(2,1)S(1)} collective-permute-done((bf16[72,1152]{1,0:T(8,128)(2,1)}, bf16[72,1152]{1,0:T(8,128)(2,1)S(1)}, u32[]{:S(2)}, u32[]{:S(2)}) %collective-permute-start.43) | collective-permute-done | bytes 165920 | tf_op jit(solution)/shard_map/ppermute | solution.py:116
  176.3 14.1 %collective-permute-done.46.refs_7_ = bf16[4,72,1152]{2,1,0:T(8,128)(2,1)} collective-permute-done((bf16[4,72,1152]{2,1,0:T(8,128)(2,1)S(1)}, bf16[4,72,1152]{2,1,0:T(8,128)(2,1)}, u32[]{:S(2)}, u32[]{:S(2)}) %collective-permute-start.46) | collective-permute-done | bytes 663584 | tf_op jit(solution)/shard_map/ppermute | solution.py:116
  197.2 7.3 %collective-permute-done.39.refs_3_ = bf16[4,72,1152]{2,1,0:T(8,128)(2,1)} collective-permute-done((bf16[4,72,1152]{2,1,0:T(8,128)(2,1)S(1)}, bf16[4,72,1152]{2,1,0:T(8,128)(2,1)}, u32[]{:S(2)}, u32[]{:S(2)}) %collective-permute-start.39) | collective-permute-done | bytes 663584 | tf_op jit(solution)/shard_map/ppermute | solution.py:116
  204.7 12.2 %collective-permute-done.40.refs_4_ = bf16[4,72,1152]{2,1,0:T(8,128)(2,1)} collective-permute-done((bf16[4,72,1152]{2,1,0:T(8,128)(2,1)}, bf16[4,72,1152]{2,1,0:T(8,128)(2,1)}, u32[]{:S(2)}, u32[]{:S(2)}) %collective-permute-start.40) | collective-permute-done | bytes 663584 | tf_op jit(solution)/shard_map/ppermute | solution.py:116
  216.9 6.8 %place.6 = bf16[32,72,1152]{2,1,0:T(8,128)(2,1)} custom-call(s32[32]{0:T(128)S(1)} %stack.809.refs_0_, bf16[4,72,1152]{2,1,0:T(8,128)(2,1)S(1)} %pad_maximum_fusion.18.refs_1_, bf16[4,72,1152]{2,1,0:T(8,128)(2,1)} %collective-permute-done.38.refs_2_, bf16[4,72,1152]{2,1,0:T(8,128)(2,1)} %collective-permute-done.39.refs_3_, ...), custom_call_target="tpu_custom_call" | custom-call | bytes 10616832 | tf_op jit(solution)/shard_map/place/pallas_call | solution.py:61
  223.7 8.6 %copy.237 = bf16[2,1152,1152]{1,2,0:T(8,128)(2,1)} copy(bf16[2,1152,1152]{2,1,0:T(8,128)(2,1)} %bitcast.556) | data formatting | bytes 10616832 | tf_op jit(solution)/shard_map/reshape | solution.py:214
  247.7 8.4 %copy.259 = bf16[2,2304,576]{2,1,0:T(8,128)(2,1)} copy(bf16[2,2304,576]{1,2,0:T(8,128)(2,1)} %fusion.1) | data formatting | bytes 10616832 | tf_op jit(solution)/shard_map/convert_element_type | solution.py:323
  256.2 11.6 %pick.7 = (bf16[4,144,576]{2,1,0:T(8,128)(2,1)S(1)}, bf16[4,144,576]{2,1,0:T(8,128)(2,1)S(1)}, bf16[4,144,576]{2,1,0:T(8,128)(2,1)S(1)}, bf16[4,144,576]{2,1,0:T...) custom-call(s32[32]{0:T(128)S(1)} %stack.974.refs_0_, ...), custom_call_target="tpu_custom_call" | custom-call | bytes 10616832 | tf_op jit(solution)/shard_map/pick/pallas_call | solution.py:78
  270.0 17.3 %collective-permute-done.98 = bf16[4,144,576]{2,1,0:T(8,128)(2,1)S(1)} collective-permute-done((bf16[4,144,576]{2,1,0:T(8,128)(2,1)S(1)}, bf16[4,144,576]{2,1,0:T(8,128)(2,1)S(1)}, u32[]{:S(2)}, u32[]{:S(2)}) %collective-permute-start.98) | collective-permute-done | bytes 663584 | tf_op jit(solution)/shard_map/ppermute | solution.py:116
  291.5 11.6 %collective-permute-done.97 = bf16[4,144,576]{2,1,0:T(8,128)(2,1)S(1)} collective-permute-done((bf16[4,144,576]{2,1,0:T(8,128)(2,1)S(1)}, bf16[4,144,576]{2,1,0:T(8,128)(2,1)S(1)}, u32[]{:S(2)}, u32[]{:S(2)}) %collective-permute-start.97) | collective-permute-done | bytes 663584 | tf_op jit(solution)/shard_map/ppermute | solution.py:116
  328.5 7.9 %collective-permute-done.107 = bf16[144,576]{1,0:T(8,128)(2,1)S(1)} collective-permute-done((bf16[144,576]{1,0:T(8,128)(2,1)S(1)}, bf16[144,576]{1,0:T(8,128)(2,1)S(1)}, u32[]{:S(2)}, u32[]{:S(2)}) %collective-permute-start.107) | collective-permute-done | bytes 165920 | tf_op jit(solution)/shard_map/ppermute | solution.py:116
  343.1 10.4 %collective-permute-done.49 = bf16[144,576]{1,0:T(8,128)(2,1)S(1)} collective-permute-done((bf16[144,576]{1,0:T(8,128)(2,1)S(1)}, bf16[144,576]{1,0:T(8,128)(2,1)S(1)}, u32[]{:S(2)}, u32[]{:S(2)}) %collective-permute-start.49) | collective-permute-done | bytes 165920 | tf_op jit(solution)/shard_map/ppermute | solution.py:116
  357.0 10.6 %collective-permute-done.55 = bf16[144,576]{1,0:T(8,128)(2,1)S(1)} collective-permute-done((bf16[144,576]{1,0:T(8,128)(2,1)S(1)}, bf16[144,576]{1,0:T(8,128)(2,1)S(1)}, u32[]{:S(2)}, u32[]{:S(2)}) %collective-permute-start.55) | collective-permute-done | bytes 165920 | tf_op jit(solution)/shard_map/ppermute | solution.py:116
  374.6 12.7 %collective-permute-done.58.refs_7_ = bf16[4,144,576]{2,1,0:T(8,128)(2,1)} collective-permute-done((bf16[4,144,576]{2,1,0:T(8,128)(2,1)S(1)}, bf16[4,144,576]{2,1,0:T(8,128)(2,1)}, u32[]{:S(2)}, u32[]{:S(2)}) %collective-permute-start.58) | collective-permute-done | bytes 663584 | tf_op jit(solution)/shard_map/ppermute | solution.py:116
  388.0 15.1 %collective-permute-done.52.refs_3_ = bf16[4,144,576]{2,1,0:T(8,128)(2,1)} collective-permute-done((bf16[4,144,576]{2,1,0:T(8,128)(2,1)S(1)}, bf16[4,144,576]{2,1,0:T(8,128)(2,1)}, u32[]{:S(2)}, u32[]{:S(2)}) %collective-permute-start.52) | collective-permute-done | bytes 663584 | tf_op jit(solution)/shard_map/ppermute | solution.py:116
  403.1 14.7 %collective-permute-done.53.refs_4_ = bf16[4,144,576]{2,1,0:T(8,128)(2,1)} collective-permute-done((bf16[4,144,576]{2,1,0:T(8,128)(2,1)}, bf16[4,144,576]{2,1,0:T(8,128)(2,1)}, u32[]{:S(2)}, u32[]{:S(2)}) %collective-permute-start.53) | collective-permute-done | bytes 663584 | tf_op jit(solution)/shard_map/ppermute | solution.py:116
  417.8 7.1 %place.7 = bf16[32,144,576]{2,1,0:T(8,128)(2,1)} custom-call(s32[32]{0:T(128)S(1)} %stack.882.refs_0_, bf16[4,144,576]{2,1,0:T(8,128)(2,1)S(1)} %pad_maximum_fusion.15.refs_1_, bf16[4,144,576]{2,1,0:T(8,128)(2,1)} %collective-permute-done.51.refs_2_, bf16[4,144,576]{2,1,0:T(8,128)(2,1)} %collective-permute-done.52.refs_3_, ...), custom_call_target="tpu_custom_call" | custom-call | bytes 10616832 | tf_op jit(solution)/shard_map/place/pallas_call | solution.py:61
  425.0 8.4 %fusion.8 = bf16[512,2304]{1,0:T(8,128)(2,1)S(1)} fusion(f32[512,2304]{1,0:T(8,128)} %copy-done.85, bf16[2,2304,576]{2,1,0:T(8,128)(2,1)} %bitcast.563, bf16[256,2,576]{0,2,1:T(8,128)(2,1)S(1)} %bitcast.576, bf16[256,2,576]{0,2,1:T(8,128)(2,1)S(1)} %bitcast.574), kind=kOutput, calls=%fused_computation.14 | convolution fusion | flops 2743861248 | bytes 13565952 | tf_op jit(solution)/shard_map/txk,xrk->tr/dot_general | solution.py:318
  433.4 7.7 %fusion.14 = f32[512,2,576]{0,2,1:T(8,128)} fusion(bf16[2,2304,576]{2,1,0:T(8,128)(2,1)S(1)} %bitcast.564, f32[512,2304]{1,0:T(8,128)} %copy-done.85), kind=kOutput, calls=%fused_computation.29 | convolution fusion | flops 2728525824 | bytes 12386304 | tf_op jit(solution)/shard_map/tr,xrk->txk/dot_general | solution.py:312
  441.1 6.2 convolution_convert_fusion
  447.4 9.7 %pick.6 = (bf16[4,72,1152]{2,1,0:T(8,128)(2,1)S(1)}, bf16[4,72,1152]{2,1,0:T(8,128)(2,1)S(1)}, bf16[4,72,1152]{2,1,0:T(8,128)(2,1)S(1)}, bf16[4,72,1152]{2,1,0:T...) custom-call(s32[32]{0:T(128)S(1)} %stack.927.refs_0_, ...), custom_call_target="tpu_custom_call" | custom-call | bytes 10616832 | tf_op jit(solution)/shard_map/pick/pallas_call | solution.py:78
  497.1 8.5 %collective-permute-done.92 = bf16[4,72,1152]{2,1,0:T(8,128)(2,1)} collective-permute-done((bf16[4,72,1152]{2,1,0:T(8,128)(2,1)}, bf16[4,72,1152]{2,1,0:T(8,128)(2,1)}, u32[]{:S(2)}, u32[]{:S(2)}) %collective-permute-start.92) | collective-permute-done | bytes 663584 | tf_op jit(solution)/shard_map/ppermute | solution.py:116
  524.8 8.7 %collective-permute-done.94 = bf16[72,1152]{1,0:T(8,128)(2,1)S(1)} collective-permute-done((bf16[72,1152]{1,0:T(8,128)(2,1)S(1)}, bf16[72,1152]{1,0:T(8,128)(2,1)S(1)}, u32[]{:S(2)}, u32[]{:S(2)}) %collective-permute-start.94) | collective-permute-done | bytes 165920 | tf_op jit(solution)/shard_map/ppermute | solution.py:116
  555.3 6.9 %convolution_bitcast_fusion.2 = f32[512,1152]{1,0:T(8,128)} fusion(bf16[512,2,864]{0,2,1:T(8,128)(2,1)} %convert_element_type.388, bf16[2,1152,864]{2,1,0:T(8,128)(2,1)} %bitcast.562), kind=kOutput, calls=%fused_computation.22 | convolution fusion | flops 2038431744 | bytes 8110080 | tf_op jit(solution)/shard_map/txk,xrk->tr/dot_general | solution.py:318
  567.9 6.3 copy.254
  574.3 7.4 %pick.4 = (bf16[4,72,864]{2,1,0:T(8,128)(2,1)S(1)}, bf16[4,72,864]{2,1,0:T(8,128)(2,1)S(1)}, bf16[4,72,864]{2,1,0:T(8,128)(2,1)S(1)}, bf16[4,72,864]{2,1,0:T(8,1...) custom-call(s32[32]{0:T(128)S(1)} %stack.927.refs_0_, ...), custom_call_target="tpu_custom_call" | custom-call | bytes 7962624 | tf_op jit(solution)/shard_map/pick/pallas_call | solution.py:78
  603.6 7.3 %collective-permute-done.72 = bf16[4,72,864]{2,1,0:T(8,128)(2,1)} collective-permute-done((bf16[4,72,864]{2,1,0:T(8,128)(2,1)}, bf16[4,72,864]{2,1,0:T(8,128)(2,1)}, u32[]{:S(2)}, u32[]{:S(2)}) %collective-permute-start.72) | collective-permute-done | bytes 497696 | tf_op jit(solution)/shard_map/ppermute | solution.py:116
  (559 shorter events, 367.8 us)
Async XLA Ops:
  2.2 44.3 %collective-permute-start.28 = (bf16[72,576]{1,0:T(8,128)(2,1)}, bf16[72,576]{1,0:T(8,128)(2,1)S(1)}, u32[]{:S(2)}, u32[]{:S(2)}) collective-permute-start(bf16[72,576]{1,0:T(8,128)(2,1)} %convert_element_type.378), channel_id=1, source_target_pairs={{0,16},{1,17},{2,18},{3,19},{4,20},{5,21},{6,22},{7,23},{8,24},{9,... | collective-permute-start | bytes 248840 | tf_op jit(solution)/shard_map/ppermute | solution.py:116
  6.3 47.6 %collective-permute-start.27 = (bf16[72,576]{1,0:T(8,128)(2,1)}, bf16[72,576]{1,0:T(8,128)(2,1)}, u32[]{:S(2)}, u32[]{:S(2)}) collective-permute-start(bf16[72,576]{1,0:T(8,128)(2,1)} %convert_element_type.378), channel_id=1, source_target_pairs={{0,8},{1,9},{2,10},{3,11},{4,12},{5,13},{6,14},{7,15},{8,16},{9,17... | collective-permute-start | bytes 248840 | tf_op jit(solution)/shard_map/ppermute | solution.py:116
  76.3 29.4 %collective-permute-start.17 = (bf16[4,72,864]{2,1,0:T(8,128)(2,1)S(1)}, bf16[4,72,864]{2,1,0:T(8,128)(2,1)}, u32[]{:S(2)}, u32[]{:S(2)}) collective-permute-start(bf16[4,72,864]{2,1,0:T(8,128)(2,1)S(1)} %pad_maximum_fusion.20.refs_1_), channel_id=1, source_target_pairs={{0,1},{1,0},{2,3},{3,2},{4,5},{5,4},{6,7},{7,6},{8,9},{9,8},{10,11... | collective-permute-start | bytes 1493000 | tf_op jit(solution)/shard_map/ppermute | solution.py:116
  77.6 54.0 %collective-permute-start.12 = (bf16[256,1152]{1,0:T(8,128)(2,1)}, bf16[256,1152]{1,0:T(8,128)(2,1)}, u32[]{:S(2)}, u32[]{:S(2)}) collective-permute-start(bf16[256,1152]{1,0:T(8,128)(2,1)} %fusion.43), channel_id=1, source_target_pairs={{0,2},{1,3},{2,0},{3,1},{4,6},{5,7},{6,4},{7,5},{8,10},{9,11},{10,... | collective-permute-start | bytes 1769480 | tf_op jit(solution)/shard_map/ppermute | solution.py:116
  80.1 27.7 %collective-permute-start.23 = (bf16[4,72,864]{2,1,0:T(8,128)(2,1)S(1)}, bf16[4,72,864]{2,1,0:T(8,128)(2,1)}, u32[]{:S(2)}, u32[]{:S(2)}) collective-permute-start(bf16[4,72,864]{2,1,0:T(8,128)(2,1)S(1)} %pad_maximum_fusion.21.refs_5_), channel_id=1, source_target_pairs={{0,4},{1,5},{2,6},{3,7},{4,0},{5,1},{6,2},{7,3},{8,12},{9,13},{10,... | collective-permute-start | bytes 1493000 | tf_op jit(solution)/shard_map/ppermute | solution.py:116
  105.6 49.1 %collective-permute-start.37 = (bf16[72,1152]{1,0:T(8,128)(2,1)}, bf16[72,1152]{1,0:T(8,128)(2,1)}, u32[]{:S(2)}, u32[]{:S(2)}) collective-permute-start(bf16[72,1152]{1,0:T(8,128)(2,1)} %select_n.1517), channel_id=1, source_target_pairs={{0,24},{1,25},{2,26},{3,27},{4,28},{5,29},{6,30},{7,31},{8,0},{9,1... | collective-permute-start | bytes 497672 | tf_op jit(solution)/shard_map/ppermute | solution.py:116
  107.8 48.5 %collective-permute-start.36 = (bf16[72,1152]{1,0:T(8,128)(2,1)}, bf16[72,1152]{1,0:T(8,128)(2,1)}, u32[]{:S(2)}, u32[]{:S(2)}) collective-permute-start(bf16[72,1152]{1,0:T(8,128)(2,1)} %select_n.1517), channel_id=1, source_target_pairs={{0,16},{1,17},{2,18},{3,19},{4,20},{5,21},{6,22},{7,23},{8,24},{9,... | collective-permute-start | bytes 497672 | tf_op jit(solution)/shard_map/ppermute | solution.py:116
  114.7 42.3 %collective-permute-start.35 = (bf16[72,1152]{1,0:T(8,128)(2,1)}, bf16[72,1152]{1,0:T(8,128)(2,1)}, u32[]{:S(2)}, u32[]{:S(2)}) collective-permute-start(bf16[72,1152]{1,0:T(8,128)(2,1)} %select_n.1517), channel_id=1, source_target_pairs={{0,8},{1,9},{2,10},{3,11},{4,12},{5,13},{6,14},{7,15},{8,16},{9,17... | collective-permute-start | bytes 497672 | tf_op jit(solution)/shard_map/ppermute | solution.py:116
  118.6 36.0 %collective-permute-start.41 = (bf16[72,1152]{1,0:T(8,128)(2,1)}, bf16[72,1152]{1,0:T(8,128)(2,1)}, u32[]{:S(2)}, u32[]{:S(2)}) collective-permute-start(bf16[72,1152]{1,0:T(8,128)(2,1)} %select_n.1519), channel_id=1, source_target_pairs={{0,2},{1,3},{2,0},{3,1},{4,6},{5,7},{6,4},{7,5},{8,10},{9,11},{10,... | collective-permute-start | bytes 497672 | tf_op jit(solution)/shard_map/ppermute | solution.py:116
  154.0 39.0 %collective-permute-start.33 = (f32[256,1152]{1,0:T(8,128)}, f32[256,1152]{1,0:T(8,128)}, u32[]{:S(2)}, u32[]{:S(2)}) collective-permute-start(f32[256,1152]{1,0:T(8,128)} %copy.233), channel_id=1, source_target_pairs={{0,2},{1,3},{2,0},{3,1},{4,6},{5,7},{6,4},{7,5},{8,10},{9,11},{10,... | collective-permute-start | bytes 3538952 | tf_op jit(solution)/shard_map/ppermute | solution.py:116
  174.0 30.5 %collective-permute-start.39 = (bf16[4,72,1152]{2,1,0:T(8,128)(2,1)S(1)}, bf16[4,72,1152]{2,1,0:T(8,128)(2,1)}, u32[]{:S(2)}, u32[]{:S(2)}) collective-permute-start(bf16[4,72,1152]{2,1,0:T(8,128)(2,1)S(1)} %pad_maximum_fusion.18.refs_1_), channel_id=1, source_target_pairs={{0,1},{1,0},{2,3},{3,2},{4,5},{5,4},{6,7},{7,6},{8,9},{9,8},{10,11... | collective-permute-start | bytes 1990664 | tf_op jit(solution)/shard_map/ppermute | solution.py:116
  174.4 30.2 %collective-permute-start.45 = (bf16[4,72,1152]{2,1,0:T(8,128)(2,1)S(1)}, bf16[4,72,1152]{2,1,0:T(8,128)(2,1)}, u32[]{:S(2)}, u32[]{:S(2)}) collective-permute-start(bf16[4,72,1152]{2,1,0:T(8,128)(2,1)S(1)} %pad_maximum_fusion.19.refs_5_), channel_id=1, source_target_pairs={{0,4},{1,5},{2,6},{3,7},{4,0},{5,1},{6,2},{7,3},{8,12},{9,13},{10,... | collective-permute-start | bytes 1990664 | tf_op jit(solution)/shard_map/ppermute | solution.py:116
  174.6 42.3 %collective-permute-start.40 = (bf16[4,72,1152]{2,1,0:T(8,128)(2,1)}, bf16[4,72,1152]{2,1,0:T(8,128)(2,1)}, u32[]{:S(2)}, u32[]{:S(2)}) collective-permute-start(bf16[4,72,1152]{2,1,0:T(8,128)(2,1)} %collective-permute-done.38.refs_2_), channel_id=1, source_target_pairs={{0,1},{1,0},{2,3},{3,2},{4,5},{5,4},{6,7},{7,6},{8,9},{9,8},{10,11... | collective-permute-start | bytes 1990664 | tf_op jit(solution)/shard_map/ppermute | solution.py:116
  195.7 36.8 %collective-permute-start.61 = (bf16[256,1152]{1,0:T(8,128)(2,1)S(1)}, bf16[256,1152]{1,0:T(8,128)(2,1)}, u32[]{:S(2)}, u32[]{:S(2)}) collective-permute-start(bf16[256,1152]{1,0:T(8,128)(2,1)S(1)} %bitcast.572), channel_id=1, source_target_pairs={{0,2},{1,3},{2,0},{3,1},{4,6},{5,7},{6,4},{7,5},{8,10},{9,11},{10,... | collective-permute-start | bytes 1769480 | tf_op jit(solution)/shard_map/ppermute | solution.py:116
  204.5 29.5 %collective-permute-start.34 = (bf16[256,1152]{1,0:T(8,128)(2,1)}, bf16[256,1152]{1,0:T(8,128)(2,1)}, u32[]{:S(2)}, u32[]{:S(2)}) collective-permute-start(bf16[256,1152]{1,0:T(8,128)(2,1)} %fusion.44), channel_id=1, source_target_pairs={{0,2},{1,3},{2,0},{3,1},{4,6},{5,7},{6,4},{7,5},{8,10},{9,11},{10,... | collective-permute-start | bytes 1769480 | tf_op jit(solution)/shard_map/ppermute | solution.py:116
  269.7 33.4 %collective-permute-start.97 = (bf16[4,144,576]{2,1,0:T(8,128)(2,1)S(1)}, bf16[4,144,576]{2,1,0:T(8,128)(2,1)S(1)}, u32[]{:S(2)}, u32[]{:S(2)}) collective-permute-start(bf16[4,144,576]{2,1,0:T(8,128)(2,1)S(1)} %get-tuple-element.66), channel_id=1, source_target_pairs={{0,1},{1,0},{2,3},{3,2},{4,5},{5,4},{6,7},{7,6},{8,9},{9,8},{10,11... | collective-permute-start | bytes 1990664 | tf_op jit(solution)/shard_map/ppermute | solution.py:116
  287.6 29.9 %collective-permute-start.103 = (bf16[4,144,576]{2,1,0:T(8,128)(2,1)S(1)}, bf16[4,144,576]{2,1,0:T(8,128)(2,1)S(1)}, u32[]{:S(2)}, u32[]{:S(2)}) collective-permute-start(bf16[4,144,576]{2,1,0:T(8,128)(2,1)S(1)} %get-tuple-element.70), channel_id=1, source_target_pairs={{0,4},{1,5},{2,6},{3,7},{4,0},{5,1},{6,2},{7,3},{8,12},{9,13},{10,... | collective-permute-start | bytes 1990664 | tf_op jit(solution)/shard_map/ppermute | solution.py:116
  289.7 27.7 %collective-permute-start.105 = (bf16[4,144,576]{2,1,0:T(8,128)(2,1)S(1)}, bf16[4,144,576]{2,1,0:T(8,128)(2,1)S(1)}, u32[]{:S(2)}, u32[]{:S(2)}) collective-permute-start(bf16[4,144,576]{2,1,0:T(8,128)(2,1)S(1)} %add_convert_fusion), channel_id=1, source_target_pairs={{0,1},{1,0},{2,3},{3,2},{4,5},{5,4},{6,7},{7,6},{8,9},{9,8},{10,11... | collective-permute-start | bytes 1990664 | tf_op jit(solution)/shard_map/ppermute | solution.py:116
  369.6 33.4 %collective-permute-start.52 = (bf16[4,144,576]{2,1,0:T(8,128)(2,1)S(1)}, bf16[4,144,576]{2,1,0:T(8,128)(2,1)}, u32[]{:S(2)}, u32[]{:S(2)}) collective-permute-start(bf16[4,144,576]{2,1,0:T(8,128)(2,1)S(1)} %pad_maximum_fusion.15.refs_1_), channel_id=1, source_target_pairs={{0,1},{1,0},{2,3},{3,2},{4,5},{5,4},{6,7},{7,6},{8,9},{9,8},{10,11... | collective-permute-start | bytes 1990664 | tf_op jit(solution)/shard_map/ppermute | solution.py:116
  369.8 33.2 %collective-permute-start.57 = (bf16[4,144,576]{2,1,0:T(8,128)(2,1)S(1)}, bf16[4,144,576]{2,1,0:T(8,128)(2,1)}, u32[]{:S(2)}, u32[]{:S(2)}) collective-permute-start(bf16[4,144,576]{2,1,0:T(8,128)(2,1)S(1)} %pad_maximum_fusion.16.refs_5_), channel_id=1, source_target_pairs={{0,4},{1,5},{2,6},{3,7},{4,0},{5,1},{6,2},{7,3},{8,12},{9,13},{10,... | collective-permute-start | bytes 1990664 | tf_op jit(solution)/shard_map/ppermute | solution.py:116
  373.0 44.9 %collective-permute-start.53 = (bf16[4,144,576]{2,1,0:T(8,128)(2,1)}, bf16[4,144,576]{2,1,0:T(8,128)(2,1)}, u32[]{:S(2)}, u32[]{:S(2)}) collective-permute-start(bf16[4,144,576]{2,1,0:T(8,128)(2,1)} %collective-permute-done.51.refs_2_), channel_id=1, source_target_pairs={{0,1},{1,0},{2,3},{3,2},{4,5},{5,4},{6,7},{7,6},{8,9},{9,8},{10,11... | collective-permute-start | bytes 1990664 | tf_op jit(solution)/shard_map/ppermute | solution.py:116
  387.3 30.6 %collective-permute-start.59 = (bf16[4,144,576]{2,1,0:T(8,128)(2,1)}, bf16[4,144,576]{2,1,0:T(8,128)(2,1)}, u32[]{:S(2)}, u32[]{:S(2)}) collective-permute-start(bf16[4,144,576]{2,1,0:T(8,128)(2,1)} %collective-permute-done.58.refs_7_), channel_id=1, source_target_pairs={{0,4},{1,5},{2,6},{3,7},{4,0},{5,1},{6,2},{7,3},{8,12},{9,13},{10,... | collective-permute-start | bytes 1990664 | tf_op jit(solution)/shard_map/ppermute | solution.py:116
  473.7 38.2 %collective-permute-start.84 = (bf16[4,72,1152]{2,1,0:T(8,128)(2,1)}, bf16[4,72,1152]{2,1,0:T(8,128)(2,1)}, u32[]{:S(2)}, u32[]{:S(2)}) collective-permute-start(bf16[4,72,1152]{2,1,0:T(8,128)(2,1)} %copy-done.10), channel_id=1, source_target_pairs={{0,1},{1,0},{2,3},{3,2},{4,5},{5,4},{6,7},{7,6},{8,9},{9,8},{10,11... | collective-permute-start | bytes 1990664 | tf_op jit(solution)/shard_map/ppermute | solution.py:116
  482.9 30.5 %collective-permute-start.86 = (bf16[4,72,1152]{2,1,0:T(8,128)(2,1)}, bf16[4,72,1152]{2,1,0:T(8,128)(2,1)}, u32[]{:S(2)}, u32[]{:S(2)}) collective-permute-start(bf16[4,72,1152]{2,1,0:T(8,128)(2,1)} %add_convert_fusion.3), channel_id=1, source_target_pairs={{0,4},{1,5},{2,6},{3,7},{4,0},{5,1},{6,2},{7,3},{8,12},{9,13},{10,... | collective-permute-start | bytes 1990664 | tf_op jit(solution)/shard_map/ppermute | solution.py:116
  496.6 37.7 %collective-permute-start.63 = (bf16[256,1152]{1,0:T(8,128)(2,1)S(1)}, bf16[256,1152]{1,0:T(8,128)(2,1)}, u32[]{:S(2)}, u32[]{:S(2)}) collective-permute-start(bf16[256,1152]{1,0:T(8,128)(2,1)S(1)} %fusion.143), channel_id=1, source_target_pairs={{0,2},{1,3},{2,0},{3,1},{4,6},{5,7},{6,4},{7,5},{8,10},{9,11},{10,... | collective-permute-start | bytes 1769480 | tf_op jit(solution)/shard_map/ppermute | solution.py:116
  516.8 66.0 %collective-permute-start.87 = (bf16[72,1152]{1,0:T(8,128)(2,1)}, bf16[72,1152]{1,0:T(8,128)(2,1)}, u32[]{:S(2)}, u32[]{:S(2)}) collective-permute-start(bf16[72,1152]{1,0:T(8,128)(2,1)} %get-tuple-element.146), channel_id=1, source_target_pairs={{0,8},{1,9},{2,10},{3,11},{4,12},{5,13},{6,14},{7,15},{8,16},{9,17... | collective-permute-start | bytes 497672 | tf_op jit(solution)/shard_map/ppermute | solution.py:116
  518.9 65.0 %collective-permute-start.89 = (bf16[72,1152]{1,0:T(8,128)(2,1)}, bf16[72,1152]{1,0:T(8,128)(2,1)}, u32[]{:S(2)}, u32[]{:S(2)}) collective-permute-start(bf16[72,1152]{1,0:T(8,128)(2,1)} %get-tuple-element.147), channel_id=1, source_target_pairs={{0,24},{1,25},{2,26},{3,27},{4,28},{5,29},{6,30},{7,31},{8,0},{9,1... | collective-permute-start | bytes 497672 | tf_op jit(solution)/shard_map/ppermute | solution.py:116
  520.6 64.2 %collective-permute-start.88 = (bf16[72,1152]{1,0:T(8,128)(2,1)}, bf16[72,1152]{1,0:T(8,128)(2,1)}, u32[]{:S(2)}, u32[]{:S(2)}) collective-permute-start(bf16[72,1152]{1,0:T(8,128)(2,1)} %get-tuple-element.148), channel_id=1, source_target_pairs={{0,16},{1,17},{2,18},{3,19},{4,20},{5,21},{6,22},{7,23},{8,24},{9,... | collective-permute-start | bytes 497672 | tf_op jit(solution)/shard_map/ppermute | solution.py:116
  534.2 51.0 %collective-permute-start.96 = (f32[72,1152]{1,0:T(8,128)}, f32[72,1152]{1,0:T(8,128)}, u32[]{:S(2)}, u32[]{:S(2)}) collective-permute-start(f32[72,1152]{1,0:T(8,128)} %fusion.60), channel_id=1, source_target_pairs={{0,2},{1,3},{2,0},{3,1},{4,6},{5,7},{6,4},{7,5},{8,10},{9,11},{10,... | collective-permute-start | bytes 995336 | tf_op jit(solution)/shard_map/ppermute | solution.py:116
  550.0 63.3 %collective-permute-start.78 = (bf16[4,72,576]{2,1,0:T(8,128)(2,1)}, bf16[4,72,576]{2,1,0:T(8,128)(2,1)}, u32[]{:S(2)}, u32[]{:S(2)}) collective-permute-start(bf16[4,72,576]{2,1,0:T(8,128)(2,1)} %get-tuple-element.54), channel_id=1, source_target_pairs={{0,1},{1,0},{2,3},{3,2},{4,5},{5,4},{6,7},{7,6},{8,9},{9,8},{10,11... | collective-permute-start | bytes 995336 | tf_op jit(solution)/shard_map/ppermute | solution.py:116
  584.0 38.4 %collective-permute-start.66 = (bf16[4,72,864]{2,1,0:T(8,128)(2,1)}, bf16[4,72,864]{2,1,0:T(8,128)(2,1)}, u32[]{:S(2)}, u32[]{:S(2)}) collective-permute-start(bf16[4,72,864]{2,1,0:T(8,128)(2,1)} %get-tuple-element.48), channel_id=1, source_target_pairs={{0,1},{1,0},{2,3},{3,2},{4,5},{5,4},{6,7},{7,6},{8,9},{9,8},{10,11... | collective-permute-start | bytes 1493000 | tf_op jit(solution)/shard_map/ppermute | solution.py:116
  584.8 45.2 %collective-permute-start.71 = (bf16[4,72,864]{2,1,0:T(8,128)(2,1)}, bf16[4,72,864]{2,1,0:T(8,128)(2,1)}, u32[]{:S(2)}, u32[]{:S(2)}) collective-permute-start(bf16[4,72,864]{2,1,0:T(8,128)(2,1)} %get-tuple-element.50), channel_id=1, source_target_pairs={{0,4},{1,5},{2,6},{3,7},{4,0},{5,1},{6,2},{7,3},{8,12},{9,13},{10,... | collective-permute-start | bytes 1493000 | tf_op jit(solution)/shard_map/ppermute | solution.py:116
  (171 other events, 2221.5 us)
